TPU v7x, 256 devices: a whole 4x4x8 slice. The times are simulated.
256 devices in a mesh: lat: 64 (over z, x, y_lo), lev: 4 (over y_hi, core).
Axes of the slice: x: 4, y: 4 (y_hi: 2, y_lo: 2; y = y_hi * 2 + y_lo), z: 8, core: 2. Of those that a mesh axis runs over, the one named last changes fastest.
Arguments:
- tracers: float32 [8, 8, 768, 1152], P(None, 'lev', 'lat'), may hold values from -6 to 6
- courant_x: float32 [8, 768, 1152], P('lev', 'lat'), may hold values from -0.95 to 0.95
- courant_y: float32 [8, 768, 1152], P('lev', 'lat'), may hold values from -0.95 to 0.95
- thickness: float32 [8, 768, 1152], P('lev', 'lat'), may hold values from 0.5 to 1.5
- level_weights: float32 [8], replicated, may hold values from 0.5 to 2
- surface_geo: float32 [768, 1152], P('lat'), may hold values from -6 to 6
Outputs:
- remapped: float32 [8, 8, 768, 1152], P(None, 'lev', 'lat')
- geopotential: float32 [8, 768, 1152], P('lev', 'lat')
All inputs are finite; a program needn't handle non-finite values.
Results may differ from a plain program's by a relative error of at most 0.0003.
Values sent between devices are 32-bit elements; how exact they have to be, the bound alone decides.
A program may use at most 64 MiB of HBM per device.

v0:
```python
import functools

import jax
import jax.numpy as jnp
from jax import lax
from jax.experimental import pallas as pl
from jax.experimental.pallas import tpu as pltpu
from jax.sharding import PartitionSpec as P

SUBSTEPS = 4
HALO = 3
LANES = 128
TOP_PRESSURE = 1.0
GAS_FACTOR = 0.3


def face_weights(courant):
    size = jnp.abs(courant)
    rest = 1.0 - size
    scaled = courant * rest * (1.0 / 12.0)
    return scaled * rest, scaled * size, courant * size * (3.0 - 2.0 * size)


def stencil_weights(courant):
    p, q, r = face_weights(courant)
    pos = courant > 0.0
    qp, rp = jnp.where(pos, q, 0.0), jnp.where(pos, r, 0.0)
    qn, rn = q - qp, r - rp
    p7 = 7.0 * p
    return [
        qp,
        -p - 7.0 * qp,
        p7 - 7.0 * qp + qn + rp,
        p7 + qp - 7.0 * qn + rn,
        -p - 7.0 * qn,
        qn,
    ]


def kernel(nsuper, rows, nlon, tr, cx, cy, th, wts, sgeo, out, geo,
           send1, recv1, field, zon, wz, wy, cyrow, cytop, thp, thr, col, outp, outr, geop, geor,
           s1, r1, sth, rth, sh, rh, sc, rc, sx, rx, so, ro, sg, rg):
    lat, lev = lax.axis_index("lat"), lax.axis_index("lev")
    sb, l = lat // 2, lat % 2
    h, c = lev // 2, lev % 2
    y = 2 * h + l
    tiles = nlon // LANES
    pieces = [(0, 8), (8, rows - 8)]
    has_low, has_up = sb > 0, sb < nsuper - 1

    def lane(i):
        return pl.ds(pl.multiple_of(i * LANES, LANES), LANES)

    barrier = pltpu.get_barrier_semaphore()
    for k in range(1, 8):
        pl.semaphore_signal(barrier, 1, device_id=(2 * sb + (l ^ (k // 4)), lev ^ (k % 4)))

    @pl.when(has_low)
    def _():
        pl.semaphore_signal(barrier, 1, device_id=(lat - 2, lev))

    @pl.when(has_up)
    def _():
        pl.semaphore_signal(barrier, 1, device_id=(lat + 2, lev))

    def pack(i, _):
        at = lane(i)
        for f in range(8):
            for a in range(2):
                for r0, n in pieces:
                    send1[f // 2, i, pl.ds(r0 * 8 + 2 * (f % 2) + a, n, stride=8), :] = tr[f, a, r0:r0 + n, at]
        for arr, ref in ((2, cx), (3, cy)):
            for a in range(2):
                for r0, n in pieces:
                    piece = ref[a, r0:r0 + n, at]
                    for dest in range(4):
                        send1[dest, i, pl.ds(r0 * 8 + 2 * arr + a, n, stride=8), :] = piece
        for a in range(2):
            thp[i, a * rows:(a + 1) * rows, :] = th[a, :, at]
        return 0

    lax.fori_loop(0, tiles, pack, 0)

    @pl.when(jnp.logical_not(has_low))
    def _():
        for t in range(SUBSTEPS):
            zon[t, :, 0:8 * HALO, :] = jnp.zeros((tiles, 8 * HALO, LANES), jnp.float32)

    @pl.when(jnp.logical_not(has_up))
    def _():
        for t in range(SUBSTEPS):
            zon[t, :, 8 * (HALO + 2 * rows):, :] = jnp.zeros((tiles, 8 * HALO, LANES), jnp.float32)
        cytop[...] = jnp.zeros((tiles, 8, LANES), jnp.float32)

    others = 7 + has_low.astype(jnp.int32) + has_up.astype(jnp.int32)
    pl.semaphore_wait(barrier, others)

    def copy_to(src, dst, ssem, rsem, device):
        return pltpu.make_async_remote_copy(src, dst, ssem, rsem, device_id=device)

    def start(own, src, dst, ssem, rsem, device):
        if own is None:
            copy_to(src, dst, ssem, rsem, device).start()
            return

        @pl.when(own)
        def _():
            pltpu.make_async_copy(src, dst, rsem).start()

        @pl.when(jnp.logical_not(own))
        def _():
            copy_to(src, dst, ssem, rsem, device).start()

    def sent(own, src, dst, ssem, rsem, device):
        if own is None:
            copy_to(src, dst, ssem, rsem, device).wait_send()
            return

        @pl.when(jnp.logical_not(own))
        def _():
            copy_to(src, dst, ssem, rsem, device).wait_send()

    def arrived(dst, rsem):
        pltpu.make_async_copy(dst, dst, rsem).wait()

    moves1, movesth = [], []
    for k in (3, 2, 1, 0):
        hd, ld = h ^ (k // 2), l ^ (k % 2)
        own = None if k else (c == h)
        moves1.append((own, send1.at[2 * hd + ld], recv1.at[2 * l + c], s1.at[k], r1.at[2 * l + c],
                       (2 * sb + ld, 2 * hd + h)))
        own = None if k else (c == l)
        movesth.append((own, thp, thr.at[lev], sth.at[k], rth.at[lev], (2 * sb + ld, 2 * hd + l)))
    for move in moves1:
        start(*move)
    for move in movesth:
        start(*move)

    for slot in range(4):
        arrived(recv1.at[slot], r1.at[slot])

    sub = lax.broadcasted_iota(jnp.int32, (8, LANES), 0)
    col_id = lax.broadcasted_iota(jnp.int32, (8, LANES), 1)
    keep = jnp.where(has_low, 1.0, 0.0)

    def shifted(values, steps):
        count = len(values)
        turned = [pltpu.roll(v, (-steps) % LANES, 1) for v in values]
        if steps < 0:
            return [jnp.where(col_id < -steps, turned[m - 1], turned[m]) for m in range(count)]
        return [jnp.where(col_id >= LANES - steps, turned[(m + 1) % count], turned[m]) for m in range(count)]

    def unpack(r, _):
        at8 = pl.ds(pl.multiple_of(8 * r, 8), 8)
        for band in range(2):
            to8 = pl.ds(pl.multiple_of(8 * (r + band * rows), 8), 8)
            cxs = []
            for m in range(tiles):
                b0, b1 = recv1[2 * band, m, at8, :], recv1[2 * band + 1, m, at8, :]
                half = pltpu.roll(b0, 4, 0)
                field[0, m, to8, :] = jnp.where(sub < 4, b0, pltpu.roll(b1, 4, 0))
                cxs.append(jnp.where(sub < 2, half, jnp.where(sub < 4, pltpu.roll(b0, 6, 0),
                                                              jnp.where(sub < 6, b1, pltpu.roll(b1, 2, 0)))))
                cyr = jnp.where(sub < 2, pltpu.roll(b0, 2, 0),
                                jnp.where(sub < 4, half, jnp.where(sub < 6, pltpu.roll(b1, 6, 0), b1)))
                if band == 0:
                    cyr = jnp.where(r == 0, keep * cyr, cyr)

                    @pl.when(r == 0)
                    def _():
                        cyrow[m] = cyr
                for n, w in enumerate(face_weights(cyr)):
                    wy[n, m, to8, :] = w
            for m, (cxr, cxe) in enumerate(zip(cxs, shifted(cxs, 1))):
                west, east = stencil_weights(cxr), stencil_weights(cxe)
                wz[0, m, to8, :] = west[0]
                for n in range(1, 6):
                    w = west[n] - east[n - 1]
                    wz[n, m, to8, :] = w + 1.0 if n == 3 else w
                wz[6, m, to8, :] = -east[5]
        return 0

    lax.fori_loop(0, rows, unpack, 0)

    def low_row():
        return copy_to(cyrow, cytop, sc, rc, (lat - 2, lev))

    @pl.when(has_low)
    def _():
        low_row().start()

    def zonal(t, r0, n, step):
        def do(i, _):
            for d in range(step):
                row = r0 + i * step + d
                at8 = pl.ds(pl.multiple_of(8 * row, 8), 8)
                f = [field[t, m, at8, :] for m in range(tiles)]
                total = [wz[3, m, at8, :] * f[m] for m in range(tiles)]
                for k in (0, 1, 2, 4, 5, 6):
                    moved = shifted(f, k - 3)
                    total = [total[m] + wz[k, m, at8, :] * moved[m] for m in range(tiles)]
                to8 = pl.ds(pl.multiple_of(8 * (row + HALO), 8), 8)
                for m in range(tiles):
                    zon[t, m, to8, :] = total[m]
            return 0
        lax.fori_loop(0, n // step, do, 0)

    def meridional(t, r0, n):
        def do(i, _):
            def z(row):
                return zon[t, i, 8 * (row + HALO):8 * (row + HALO) + 8, :]

            window = [z(r0 + d) for d in range(-3, 3)]
            sums = [window[m] + window[m + 1] for m in range(5)]
            def face(m):
                return 8.0 * sums[m] - (sums[m - 1] + sums[m + 1])
            values = [face(1), face(2), face(3)]
            before = None
            for row in range(r0, r0 + n + 1):
                at8 = slice(8 * row, 8 * row + 8)
                p, q, r = wy[0, i, at8, :], wy[1, i, at8, :], wy[2, i, at8, :]
                pos = p > 0.0
                flux = p * values[1] - q * jnp.where(pos, values[0], values[2]) + r * jnp.where(
                    pos, window[2], window[3])
                if before is not None:
                    field[t + 1, i, 8 * (row - 1):8 * row, :] = window[2] - (flux - before)
                before = flux
                if row < r0 + n:
                    window = window[1:] + [z(row + 3)]
                    sums = sums[1:] + [window[4] + window[5]]
                    values = values[1:] + [face(3)]
            return 0
        lax.fori_loop(0, tiles, do, 0)

    edge = 8 * HALO
    top = 8 * 2 * rows

    def to_low(t):
        return copy_to(zon.at[t, :, pl.ds(edge, edge)], zon.at[t, :, pl.ds(edge + top, edge)],
                       sh.at[t, 0], rh.at[t, 0], (lat - 2, lev))

    def to_up(t):
        return copy_to(zon.at[t, :, pl.ds(top, edge)], zon.at[t, :, pl.ds(0, edge)],
                       sh.at[t, 1], rh.at[t, 1], (lat + 2, lev))

    def edges(t):
        zonal(t, 0, HALO, HALO)

        @pl.when(has_low)
        def _():
            to_low(t).start()
        zonal(t, 2 * rows - HALO, HALO, HALO)

        @pl.when(has_up)
        def _():
            to_up(t).start()

    edges(0)
    for t in range(SUBSTEPS):
        zonal(t, HALO, 2 * rows - 2 * HALO, 3)
        if t == 0:
            @pl.when(has_up)
            def _():
                low_row().wait_recv()
            for n, w in enumerate(face_weights(cytop[...])):
                wy[n, :, top:top + 8, :] = w
        meridional(t, HALO, 2 * rows - 2 * HALO)

        @pl.when(has_low)
        def _():
            to_up(t).wait_recv()
        meridional(t, 0, HALO)

        @pl.when(has_up)
        def _():
            to_low(t).wait_recv()
        meridional(t, 2 * rows - HALO, HALO)
        if t + 1 < SUBSTEPS:
            edges(t + 1)

    part = 8 * rows
    swap = copy_to(field.at[SUBSTEPS, :, pl.ds(pl.multiple_of((1 - c) * part, part), part)], col.at[c],
                   sx, rx, (lat, lev ^ 1))
    swap.start()
    col[c] = field[SUBSTEPS, :, pl.ds(pl.multiple_of(c * part, part), part), :]
    for slot in range(4):
        arrived(thr.at[slot], rth.at[slot])
    swap.wait_recv()

    def remap(i, _):
        for r0, n in pieces:
            shape = (n, LANES)
            weights = [jnp.full(shape, wts[k], jnp.float32) for k in range(8)]
            whole = weights[0]
            for k in range(1, 8):
                whole = whole + weights[k]
            inverse = 1.0 / whole
            thick = [thr[j // 2, i, (j % 2) * rows + r0:(j % 2) * rows + r0 + n, :] for j in range(8)]
            bounds = [jnp.full(shape, TOP_PRESSURE, jnp.float32)]
            for j in range(8):
                bounds.append(bounds[-1] + thick[j])
            span = bounds[8] - TOP_PRESSURE
            low, up, total = [], [], None
            for k in range(8):
                total = weights[k] if total is None else total + weights[k]
                low.append(TOP_PRESSURE + span * (total * inverse))
                up.append(low[k] - span * (weights[k] * inverse))
            density = [[], []]
            for j in range(8):
                reciprocal = 1.0 / thick[j]
                for f in range(2):
                    sublane = 4 * ((j % 4) // 2) + 2 * f + j % 2
                    density[f].append(col[j // 4, i, pl.ds(r0 * 8 + sublane, n, stride=8), :] * reciprocal)
            for k in range(8):
                sums = [None, None]
                for j in range(8):
                    cut = jnp.maximum(0.0, jnp.minimum(bounds[j + 1], low[k]) - jnp.maximum(bounds[j], up[k]))
                    for f in range(2):
                        term = density[f][j] * cut
                        sums[f] = term if sums[f] is None else sums[f] + term
                for f in range(2):
                    outp[k // 2, i, pl.ds(r0 * 4 + 2 * f + k % 2, n, stride=4), :] = sums[f]
                density_k = sums[0]
                low_k = low[k]
                up_k = up[k]

                @pl.when(y == 0)
                def _():
                    geop[k // 2, i, (k % 2) * rows + r0:(k % 2) * rows + r0 + n, :] = (
                        GAS_FACTOR * density_k / (low_k - up_k) * jnp.log(low_k / up_k))
        return 0

    lax.fori_loop(0, tiles, remap, 0)

    moves2, movesg = [], []
    for k in (3, 2, 1, 0):
        gd = lev ^ k
        moves2.append((None if k else (c == l), outp.at[gd], outr.at[y], so.at[k], ro.at[y], (2 * sb + c, gd)))
        movesg.append((None if k else (c == l), geop.at[gd], geor, sg.at[k], rg, (2 * sb + c, gd)))
    for move in moves2:
        start(*move)

    @pl.when(y == 0)
    def _():
        def integrate(i, _):
            total = None
            for k in range(7, -1, -1):
                here = slice((k % 2) * rows, (k % 2) * rows + rows)
                layer = geop[k // 2, i, here, :]
                total = layer if total is None else total + layer
                geop[k // 2, i, here, :] = total
            return 0
        lax.fori_loop(0, tiles, integrate, 0)
        for move in movesg:
            start(*move)

    for slot in range(4):
        arrived(outr.at[slot], ro.at[slot])

    def finish(i, _):
        at = lane(i)
        for f in range(8):
            for a in range(2):
                for r0, n in pieces:
                    out[f, a, r0:r0 + n, at] = outr[f // 2, i, pl.ds(r0 * 4 + 2 * (f % 2) + a, n, stride=4), :]
        return 0

    lax.fori_loop(0, tiles, finish, 0)
    arrived(geor, rg)

    def finish_geo(i, _):
        at = lane(i)
        for a in range(2):
            geo[a, :, at] = geor[i, a * rows:(a + 1) * rows, :] + sgeo[:, at]
        return 0

    lax.fori_loop(0, tiles, finish_geo, 0)

    for move in moves1 + movesth + moves2:
        sent(*move)

    @pl.when(y == 0)
    def _():
        for move in movesg:
            sent(*move)
    swap.wait_send()

    @pl.when(has_low)
    def _():
        low_row().wait_send()
        for t in range(SUBSTEPS):
            to_low(t).wait_send()

    @pl.when(has_up)
    def _():
        for t in range(SUBSTEPS):
            to_up(t).wait_send()


def body(nsuper, tracers, courant_x, courant_y, thickness, level_weights, surface_geo):
    rows, nlon = tracers.shape[2:]
    f32 = jnp.float32
    vmem = pl.BlockSpec(memory_space=pltpu.VMEM)

    def buffer(count, height):
        return pltpu.VMEM((count, nlon // LANES, height, LANES), f32)

    def single(height):
        return pltpu.VMEM((nlon // LANES, height, LANES), f32)

    dma = pltpu.SemaphoreType.DMA
    both = 2 * rows
    scratch = [
        buffer(4, 8 * rows), buffer(4, 8 * rows), buffer(SUBSTEPS + 1, 8 * both),
        buffer(SUBSTEPS, 8 * (both + 2 * HALO)), buffer(7, 8 * both), buffer(3, 8 * (both + 1)),
        single(8), single(8), single(both), buffer(4, both), buffer(2, 8 * rows),
        buffer(4, 4 * rows), buffer(4, 4 * rows), buffer(4, both), single(both),
        dma((4,)), dma((4,)), dma((4,)), dma((4,)), dma((SUBSTEPS, 2)), dma((SUBSTEPS, 2)), dma, dma, dma, dma,
        dma((4,)), dma((4,)), dma((4,)), dma,
    ]
    return pl.pallas_call(
        functools.partial(kernel, nsuper, rows, nlon),
        out_shape=(jax.ShapeDtypeStruct(tracers.shape, f32), jax.ShapeDtypeStruct(thickness.shape, f32)),
        in_specs=[vmem] * 4 + [pl.BlockSpec(memory_space=pltpu.SMEM), vmem],
        out_specs=(vmem, vmem),
        scratch_shapes=scratch,
        compiler_params=pltpu.CompilerParams(
            collective_id=0, has_side_effects=True, vmem_limit_bytes=50 * 2**20),
        name="transport_remap",
    )(tracers, courant_x, courant_y, thickness, level_weights, surface_geo)


def solution(mesh):
    in_specs = (
        P(None, "lev", "lat", None),
        P("lev", "lat", None),
        P("lev", "lat", None),
        P("lev", "lat", None),
        P(),
        P("lat", None),
    )
    out_specs = (P(None, "lev", "lat", None), P("lev", "lat", None))
    run = functools.partial(body, mesh.shape["lat"] // 2)
    return jax.shard_map(run, mesh=mesh, in_specs=in_specs, out_specs=out_specs, check_vma=False)
```

profile of v0, /device:TPU:111, one launch (start us, length us, event | category | flops | bytes accessed | tf_op | source)
XLA Modules:
  0.0 81.7 jit_solution(16005100975245151220)
XLA Ops:
  0.6 0.9 %copy.9.cx = f32[2,12,1152]{2,1,0:T(8,128)S(1)} copy(f32[2,12,1152]{2,0,1:T(2,128)} %param.7) | data formatting | bytes 221184 | tf_op args[1]
  1.5 0.9 %copy.10.cy = f32[2,12,1152]{2,1,0:T(8,128)S(1)} copy(f32[2,12,1152]{2,0,1:T(2,128)} %param.8) | data formatting | bytes 221184 | tf_op args[2]
  2.5 0.0 copy-start
  2.5 0.0 copy-start.1
  2.5 0.9 %copy.11.th = f32[2,12,1152]{2,1,0:T(8,128)S(1)} copy(f32[2,12,1152]{2,0,1:T(2,128)} %param.9) | data formatting | bytes 221184 | tf_op args[3]
  3.4 1.3 %copy.8.tr = f32[8,2,12,1152]{3,2,1,0:T(8,128)S(1)} copy(f32[8,2,12,1152]{3,1,2,0:T(2,128)} %param.6) | data formatting | bytes 1769472 | tf_op args[0]
  4.7 0.0 copy-done
  4.7 0.0 copy-done.1
  4.7 74.9 %transport_remap.1 = (f32[8,2,12,1152]{3,2,1,0:T(8,128)S(1)}, f32[2,12,1152]{2,1,0:T(8,128)S(1)}) custom-call(f32[8,2,12,1152]{3,2,1,0:T(8,128)S(1)} %copy.8.tr, f32[2,12,1152]{2,1,0:T(8,128)S(1)} %copy.9.cx, f32[2,12,1152]{2,1,0:T(8,128)S(1)} %copy.10.cy, f32[2,12,1152]{2,1,0:T(8,128)S(1)} %copy.11.th, f32[8]{0:T(128)S(1)} %copy-done.1, f32[12,1152]{1,0:T(8,128)S(1)} %copy-done), custom_call_target="tpu_custom_call" | custom-call | tf_op jit(solution)/shard_map/transport_remap/pallas_call | solution.py:421
  79.6 1.4 %copy.12 = f32[8,2,12,1152]{3,1,2,0:T(2,128)} copy(f32[8,2,12,1152]{3,2,1,0:T(8,128)S(1)} %get-tuple-element.2) | data formatting | bytes 1769472 | tf_op jit(solution)/shard_map/transport_remap/pallas_call | solution.py:421
  81.0 0.7 copy.13
Async XLA Ops:
  2.5 2.3 %copy-start = (f32[12,1152]{1,0:T(8,128)S(1)}, f32[12,1152]{1,0:T(8,128)}, u32[]{:S(2)}) copy-start(f32[12,1152]{1,0:T(8,128)} %sgeo.1) | copy-start | bytes 165892
  2.5 2.3 %copy-start.1 = (f32[8]{0:T(128)S(1)}, f32[8]{0:T(128)}, u32[]{:S(2)}) copy-start(f32[8]{0:T(128)} %wts.1) | copy-start | bytes 100
where the time goes:
time: 81.9 us; the launch traced here: 81.7 us
  Pallas kernels  74.9 us (91%)
  local copies, waits for them, and re-layouts  6.14 us (7%)
    pallas_call x1, Pallas kernels, body(): pl.pallas_call(functools.partial(kernel, nsuper, rows, nlon), out_shape=(...  74.9 us
    unnamed x8, local copies, waits for them, and re-layouts  4.07 us
    pallas_call x2, local copies, waits for them, and re-layouts, body(): pl.pallas_call(functools.partial(kernel, nsuper, rows, nlon), out_shape=(...  2.07 us

commit v1 on v0

v1 whole, which is shorter than its diff:
```python
import functools

import jax
import jax.numpy as jnp
from jax import lax
from jax.experimental import pallas as pl
from jax.experimental.layout import Layout, with_layout_constraint
from jax.experimental.pallas import tpu as pltpu
from jax.sharding import PartitionSpec as P

SUBSTEPS = 4
HALO = 3
CHUNK = 4
LANES = 128
TOP_PRESSURE = 1.0
GAS_FACTOR = 0.3


def face_weights(courant):
    size = jnp.abs(courant)
    rest = 1.0 - size
    scaled = courant * rest * (1.0 / 12.0)
    return scaled * rest, scaled * size, courant * size * (3.0 - 2.0 * size)


def stencil_weights(courant):
    p, q, r = face_weights(courant)
    pos = courant > 0.0
    qp, rp = jnp.where(pos, q, 0.0), jnp.where(pos, r, 0.0)
    qn, rn = q - qp, r - rp
    p7 = 7.0 * p
    return [
        qp,
        -p - 7.0 * qp,
        p7 - 7.0 * qp + qn + rp,
        p7 + qp - 7.0 * qn + rn,
        -p - 7.0 * qn,
        qn,
    ]


def kernel(nsuper, rows, tiles, tr, cx, cy, th, wts_hbm, out, geor, wts, lsem,
           recvf, recvx, recvy, thr, field, zon, cxt, cyt, wz, wy, cyrow, cytop, tht, col, tmp, outp, geop,
           s1, r1, sth, rth, sh, rh, sc, rc, sx, rx, so, ro, sg, rg):
    lat, lev = lax.axis_index("lat"), lax.axis_index("lev")
    sb, l = lat // 2, lat % 2
    h, c = lev // 2, lev % 2
    y = 2 * h + l
    both = 2 * rows
    chunks = rows // CHUNK
    pitch = 2 * tiles
    lines = CHUNK * pitch
    has_low, has_up = sb > 0, sb < nsuper - 1

    weights_copy = pltpu.make_async_copy(wts_hbm, wts, lsem)
    weights_copy.start()

    barrier = pltpu.get_barrier_semaphore()
    for k in range(1, 8):
        pl.semaphore_signal(barrier, 1, device_id=(2 * sb + (l ^ (k // 4)), lev ^ (k % 4)))

    @pl.when(has_low)
    def _():
        pl.semaphore_signal(barrier, 1, device_id=(lat - 2, lev))

    @pl.when(has_up)
    def _():
        pl.semaphore_signal(barrier, 1, device_id=(lat + 2, lev))

    @pl.when(jnp.logical_not(has_low))
    def _():
        for t in range(SUBSTEPS):
            zon[t, :, 0:8 * HALO, :] = jnp.zeros((tiles, 8 * HALO, LANES), jnp.float32)

    @pl.when(jnp.logical_not(has_up))
    def _():
        for t in range(SUBSTEPS):
            zon[t, :, 8 * (HALO + both):, :] = jnp.zeros((tiles, 8 * HALO, LANES), jnp.float32)
        cytop[...] = jnp.zeros((tiles, 8, LANES), jnp.float32)

    others = 7 + has_low.astype(jnp.int32) + has_up.astype(jnp.int32)
    pl.semaphore_wait(barrier, others)

    def copy_to(src, dst, ssem, rsem, device):
        return pltpu.make_async_remote_copy(src, dst, ssem, rsem, device_id=device)

    def start(own, src, dst, ssem, rsem, device):
        if own is None:
            copy_to(src, dst, ssem, rsem, device).start()
            return

        @pl.when(own)
        def _():
            pltpu.make_async_copy(src, dst, rsem).start()

        @pl.when(jnp.logical_not(own))
        def _():
            copy_to(src, dst, ssem, rsem, device).start()

    def sent(own, src, dst, ssem, rsem, device):
        if own is None:
            copy_to(src, dst, ssem, rsem, device).wait_send()
            return

        @pl.when(jnp.logical_not(own))
        def _():
            copy_to(src, dst, ssem, rsem, device).wait_send()

    def arrived(dst, rsem):
        pltpu.make_async_copy(dst, dst, rsem).wait()

    def place(band, j):
        if isinstance(band, int):
            return j * CHUNK if band == 0 else rows - (j + 1) * CHUNK
        return jnp.where(band == 0, j * CHUNK, rows - (j + 1) * CHUNK)

    def span_of(band, j):
        first = place(band, j) * pitch
        return pl.ds(first if isinstance(first, int) else pl.multiple_of(first, 8), lines)

    moves = []
    slot = 2 * l + c
    for j in range(chunks):
        here = span_of(l, j)
        groups = [[], [], []]
        for k in (3, 2, 1, 0):
            hd, ld = h ^ (k // 2), l ^ (k % 2)
            own = None if k else (c == h)
            device = (2 * sb + ld, 2 * hd + h)
            groups[0].append((own, tr.at[pl.ds(2 * (2 * hd + ld), 2), here], recvf.at[slot, :, here],
                              s1.at[0, j, k], r1.at[0, j, slot], device))
            groups[1].append((own, cx.at[here], recvx.at[slot, here], s1.at[1, j, k], r1.at[1, j, slot], device))
            groups[2].append((own, cy.at[here], recvy.at[slot, here], s1.at[2, j, k], r1.at[2, j, slot], device))
        for group in groups:
            moves += group
    for k in (3, 2, 1, 0):
        hd, ld = h ^ (k // 2), l ^ (k % 2)
        own = None if k else (c == l)
        moves.append((own, th, thr.at[lev], sth.at[k], rth.at[lev], (2 * sb + ld, 2 * hd + l)))
    for move in moves:
        start(*move)

    weights_copy.wait()

    col_id = lax.broadcasted_iota(jnp.int32, (8, LANES), 1)
    keep = jnp.where(has_low, 1.0, 0.0)

    def shifted(values, steps):
        count = len(values)
        turned = [pltpu.roll(v, (-steps) % LANES, 1) for v in values]
        if steps < 0:
            return [jnp.where(col_id < -steps, turned[m - 1], turned[m]) for m in range(count)]
        return [jnp.where(col_id >= LANES - steps, turned[(m + 1) % count], turned[m]) for m in range(count)]

    def unpack(j, source, target, twice):
        def do(i, _):
            for band in range(2):
                r0 = place(band, j)
                for pair in range(2):
                    for a in range(2):
                        for f in range(2):
                            line = pl.ds(r0 * pitch + 2 * i + a, CHUNK, stride=pitch)
                            ref = source.at[2 * band + pair] if twice else source.at[2 * band + pair, f]
                            target[i, pl.ds(8 * (band * rows + r0) + 4 * f + 2 * pair + a, CHUNK, stride=8), :] = ref[line, :]
            return 0
        lax.fori_loop(0, tiles, do, 0)

    def both_places(j):
        return [place(0, j), rows + place(1, j)]

    def at_row(row):
        return pl.ds(8 * row if isinstance(row, int) else pl.multiple_of(8 * row, 8), 8)

    def zonal_weights(j):
        def do(d, _):
            for first in both_places(j):
                at8 = at_row(first + d)
                cxs = [cxt[m, at8, :] for m in range(tiles)]
                for m, (cxr, cxe) in enumerate(zip(cxs, shifted(cxs, 1))):
                    west, east = stencil_weights(cxr), stencil_weights(cxe)
                    wz[0, m, at8, :] = west[0]
                    for n in range(1, 6):
                        w = west[n] - east[n - 1]
                        wz[n, m, at8, :] = w + 1.0 if n == 3 else w
                    wz[6, m, at8, :] = -east[5]
            return 0
        lax.fori_loop(0, CHUNK, do, 0)

    def meridional_weights(j):
        def do(i, _):
            for first in both_places(j):
                for d in range(CHUNK):
                    at8 = at_row(first + d)
                    cyr = cyt[i, at8, :]
                    if first + d == 0:
                        cyr = keep * cyr
                        cyrow[i] = cyr
                    for n, w in enumerate(face_weights(cyr)):
                        wy[n, i, at8, :] = w
            return 0
        lax.fori_loop(0, tiles, do, 0)

    def low_row():
        return copy_to(cyrow, cytop, sc, rc, (lat - 2, lev))

    def zonal(t, starts, n, step):
        def do(i, _):
            for first in starts:
                for d in range(step):
                    row = first + i * step + d
                    at8 = at_row(row)
                    f = [field[t, m, at8, :] for m in range(tiles)]
                    total = [wz[3, m, at8, :] * f[m] for m in range(tiles)]
                    for k in (0, 1, 2, 4, 5, 6):
                        moved = shifted(f, k - 3)
                        total = [total[m] + wz[k, m, at8, :] * moved[m] for m in range(tiles)]
                    to8 = at_row(row + HALO)
                    for m in range(tiles):
                        zon[t, m, to8, :] = total[m]
            return 0
        if n == step:
            do(0, 0)
        else:
            lax.fori_loop(0, n // step, do, 0)

    def meridional(t, starts, n):
        def do(i, _):
            for r0 in starts:
                def z(row):
                    return zon[t, i, 8 * (row + HALO):8 * (row + HALO) + 8, :]

                window = [z(r0 + d) for d in range(-3, 3)]
                sums = [window[m] + window[m + 1] for m in range(5)]

                def face(m):
                    return 8.0 * sums[m] - (sums[m - 1] + sums[m + 1])
                values = [face(1), face(2), face(3)]
                before = None
                for row in range(r0, r0 + n + 1):
                    at8 = at_row(row)
                    p, q, r = wy[0, i, at8, :], wy[1, i, at8, :], wy[2, i, at8, :]
                    pos = p > 0.0
                    flux = p * values[1] - q * jnp.where(pos, values[0], values[2]) + r * jnp.where(
                        pos, window[2], window[3])
                    if before is not None:
                        field[t + 1, i, at_row(row - 1), :] = window[2] - (flux - before)
                    before = flux
                    if row < r0 + n:
                        window = window[1:] + [z(row + 3)]
                        sums = sums[1:] + [window[4] + window[5]]
                        values = values[1:] + [face(3)]
            return 0
        lax.fori_loop(0, tiles, do, 0)

    edge = 8 * HALO
    top = 8 * both
    ends = [0, both - HALO]

    def to_low(t):
        return copy_to(zon.at[t, :, pl.ds(edge, edge)], zon.at[t, :, pl.ds(edge + top, edge)],
                       sh.at[t, 0], rh.at[t, 0], (lat - 2, lev))

    def to_up(t):
        return copy_to(zon.at[t, :, pl.ds(top, edge)], zon.at[t, :, pl.ds(0, edge)],
                       sh.at[t, 1], rh.at[t, 1], (lat + 2, lev))

    def send_halo(t):
        zonal(t, ends, HALO, HALO)

        @pl.when(has_low)
        def _():
            to_low(t).start()

        @pl.when(has_up)
        def _():
            to_up(t).start()

    def wait_halo(t):
        @pl.when(has_low)
        def _():
            to_up(t).wait_recv()

        @pl.when(has_up)
        def _():
            to_low(t).wait_recv()

    def take_fields(j):
        for kind, ref in ((0, recvf), (1, recvx)):
            for s in range(4):
                for band in range(2):
                    if s // 2 == band:
                        here = span_of(band, j)
                        arrived(ref.at[s, :, here] if kind == 0 else ref.at[s, here], r1.at[kind, j, s])
        unpack(j, recvx, cxt, True)
        unpack(j, recvf, field.at[0], False)
        zonal_weights(j)

    def take_courant(j):
        for s in range(4):
            arrived(recvy.at[s, span_of(s // 2, j)], r1.at[2, j, s])
        unpack(j, recvy, cyt, True)
        meridional_weights(j)

    part = 8 * CHUNK

    def swap(j):
        theirs = pl.multiple_of(8 * ((1 - c) * rows + place(1 - c, j)), part)
        return copy_to(field.at[SUBSTEPS, :, pl.ds(theirs, part)], col.at[c, j], sx.at[j], rx.at[j], (lat, lev ^ 1))

    def send_swap(j):
        swap(j).start()
        ours = pl.multiple_of(8 * (c * rows + place(c, j)), part)
        col[c, j] = field[SUBSTEPS, :, pl.ds(ours, part), :]

    full = (8, LANES)

    def take_thickness():
        for s in range(4):
            arrived(thr.at[s], rth.at[s])

        def do(i, _):
            for j in range(chunks):
                first = place(c, j) * pitch + 2 * i
                for k in range(8):
                    piece = thr[k // 2, pl.ds(first + k % 2, CHUNK, stride=pitch), :]
                    for f in range(2):
                        tht[j, i, pl.ds(8 * k + f, CHUNK, stride=2), :] = piece
            return 0
        lax.fori_loop(0, tiles, do, 0)

    def columns(j, i):
        weights = [jnp.full(full, wts[k], jnp.float32) for k in range(8)]
        whole = weights[0]
        for k in range(1, 8):
            whole = whole + weights[k]
        inverse = 1.0 / whole
        thick = [tht[j, i, 8 * k:8 * k + 8, :] for k in range(8)]
        bounds = [jnp.full(full, TOP_PRESSURE, jnp.float32)]
        for k in range(8):
            bounds.append(bounds[-1] + thick[k])
        span = bounds[8] - TOP_PRESSURE
        low, up, total = [], [], None
        for k in range(8):
            total = weights[k] if total is None else total + weights[k]
            low.append(TOP_PRESSURE + span * (total * inverse))
            up.append(low[k] - span * (weights[k] * inverse))
        return thick, bounds, low, up

    def remap(j):
        def do(i, _):
            thick, bounds, low, up = columns(j, i)
            density = [col[k // 4, j, i, pl.ds(k % 4, 8, stride=4), :] / thick[k] for k in range(8)]
            for k in range(8):
                total = None
                for n in range(8):
                    cut = jnp.maximum(0.0, jnp.minimum(bounds[n + 1], low[k]) - jnp.maximum(bounds[n], up[k]))
                    total = density[n] * cut if total is None else total + density[n] * cut
                tmp[i, 8 * k:8 * k + 8, :] = total
            for k in range(8):
                for f in range(2):
                    outp[k // 2, j, f, pl.ds(2 * i + k % 2, CHUNK, stride=pitch), :] = (
                        tmp[i, pl.ds(8 * k + f, CHUNK, stride=2), :])
            return 0
        lax.fori_loop(0, tiles, do, 0)

    def integrate(j):
        def do(i, _):
            _, _, low, up = columns(j, i)
            total = None
            for k in range(7, -1, -1):
                layer = GAS_FACTOR * tmp[i, 8 * k:8 * k + 8, :] / (low[k] - up[k]) * jnp.log(low[k] / up[k])
                total = layer if total is None else total + layer
                tmp[i, 8 * k:8 * k + 8, :] = total
            for k in range(8):
                geop[k // 2, j, pl.ds(2 * i + k % 2, CHUNK, stride=pitch), :] = (
                    tmp[i, pl.ds(8 * k, CHUNK, stride=2), :])
            return 0
        lax.fori_loop(0, tiles, do, 0)

    def result_moves(j):
        here = span_of(c, j)
        for k in (3, 2, 1, 0):
            gd = lev ^ k
            yield (None if k else (c == l), outp.at[gd, j], out.at[pl.ds(2 * y, 2), here],
                   so.at[j, k], ro.at[j, y], (2 * sb + c, gd))

    def integral_moves(j):
        here = span_of(c, j)
        for k in (3, 2, 1, 0):
            gd = lev ^ k
            yield (None if k else (c == l), geop.at[gd, j], geor.at[here], sg.at[j, k], rg.at[j], (2 * sb + c, gd))

    def send_results(j):
        swap(j).wait_recv()
        remap(j)
        for move in result_moves(j):
            start(*move)

        @pl.when(y == 0)
        def _():
            integrate(j)
            for move in integral_moves(j):
                start(*move)

    take_fields(0)
    send_halo(0)
    zonal(0, [HALO, both - HALO - 1], 1, 1)
    take_courant(0)

    @pl.when(has_low)
    def _():
        low_row().start()

    take_fields(1)
    zonal(0, both_places(1), CHUNK, CHUNK)
    take_courant(1)

    @pl.when(has_up)
    def _():
        low_row().wait_recv()
    for n, w in enumerate(face_weights(cytop[...])):
        wy[n, :, top:top + 8, :] = w
    wait_halo(0)
    meridional(0, [0, both - 5], 5)
    send_halo(1)
    zonal(1, [HALO, both - 5], 2, 2)

    take_fields(2)
    zonal(0, both_places(2), CHUNK, CHUNK)
    take_courant(2)
    meridional(0, [5], both - 10)
    zonal(1, [5, 12], 7, 1)
    wait_halo(1)
    meridional(1, ends, HALO)
    send_halo(2)
    meridional(1, [HALO], both - 2 * HALO)
    zonal(2, [HALO], both - 2 * HALO, 6)
    meridional(2, [5], both - 10)
    zonal(3, [5, 12], 7, 1)
    meridional(3, [8], 8)
    send_swap(2)

    wait_halo(2)
    meridional(2, ends, HALO)
    send_halo(3)
    take_thickness()
    send_results(2)
    meridional(2, [HALO, both - 5], 2)
    zonal(3, [HALO, both - 5], 2, 2)
    meridional(3, [HALO, both - 8], 5)
    send_swap(1)
    send_results(1)

    wait_halo(3)
    meridional(3, ends, HALO)
    send_swap(0)
    send_results(0)

    for j in range(chunks):
        arrived(geor.at[span_of(l, j)], rg.at[j])
    for j in range(chunks):
        for s in range(4):
            arrived(out.at[pl.ds(2 * s, 2), span_of(l, j)], ro.at[j, s])

    for move in moves:
        sent(*move)
    for j in range(chunks):
        swap(j).wait_send()
        for move in result_moves(j):
            sent(*move)

    @pl.when(y == 0)
    def _():
        for j in range(chunks):
            for move in integral_moves(j):
                sent(*move)

    @pl.when(has_low)
    def _():
        low_row().wait_send()
        for t in range(SUBSTEPS):
            to_low(t).wait_send()

    @pl.when(has_up)
    def _():
        for t in range(SUBSTEPS):
            to_up(t).wait_send()


def finish(rows, tiles, result, integral, surface, out, geo, held, total, sgeo, sems, gsems):
    loads = [pltpu.make_async_copy(integral, total, gsems.at[0]), pltpu.make_async_copy(surface, sgeo, gsems.at[1])]
    takes = [pltpu.make_async_copy(result.at[f], held.at[f], sems.at[0, f]) for f in range(8)]
    gives = [pltpu.make_async_copy(held.at[f], out.at[f], sems.at[1, f]) for f in range(8)]
    for copy in loads + takes:
        copy.start()
    for copy in loads:
        copy.wait()
    pitch = 2 * tiles
    for i in range(tiles):
        for r0, n in ((0, 8), (8, rows - 8)):
            piece = sgeo[r0:r0 + n, i * LANES:(i + 1) * LANES]
            for a in range(2):
                here = pl.ds(r0 * pitch + 2 * i + a, n, stride=pitch)
                total[here, :] = total[here, :] + piece
    store = pltpu.make_async_copy(total, geo, gsems.at[2])
    store.start()
    for take, give in zip(takes, gives):
        take.wait()
        give.start()
    for copy in gives + [store]:
        copy.wait()


def in_lines(array):
    lead = array.ndim - 3
    levels, rows, nlon = array.shape[lead:]
    tiles = nlon // LANES
    split = array.reshape(array.shape[:-1] + (tiles, LANES))
    order = tuple(range(lead)) + (lead + 1, lead + 2, lead, lead + 3)
    split = with_layout_constraint(split, Layout(major_to_minor=order))
    return jnp.transpose(split, order).reshape(array.shape[:lead] + (rows * tiles * levels, LANES))


def from_lines(array, levels, rows):
    lead = array.ndim - 2
    tiles = array.shape[-2] // (levels * rows)
    split = array.reshape(array.shape[:lead] + (rows, tiles, levels, LANES))
    split = jnp.transpose(split, tuple(range(lead)) + (lead + 2, lead, lead + 1, lead + 3))
    order = tuple(range(lead)) + (lead + 1, lead + 2, lead, lead + 3)
    split = with_layout_constraint(split, Layout(major_to_minor=order))
    return split.reshape(array.shape[:lead] + (levels, rows, tiles * LANES))


def body(nsuper, tracers, courant_x, courant_y, thickness, level_weights, surface_geo):
    levels, rows, nlon = thickness.shape
    tiles = nlon // LANES
    f32 = jnp.float32
    hbm = pl.BlockSpec(memory_space=pltpu.HBM)
    both = 2 * rows
    lines = rows * tiles * levels
    chunks = rows // CHUNK

    def buffer(*shape):
        return pltpu.VMEM(shape + (LANES,), f32)

    dma = pltpu.SemaphoreType.DMA
    scratch = [
        pltpu.SMEM((8,), f32), dma,
        buffer(4, 2, lines), buffer(4, lines), buffer(4, lines), buffer(4, lines),
        buffer(SUBSTEPS + 1, tiles, 8 * both), buffer(SUBSTEPS, tiles, 8 * (both + 2 * HALO)),
        buffer(tiles, 8 * both), buffer(tiles, 8 * both),
        buffer(7, tiles, 8 * both), buffer(3, tiles, 8 * (both + 1)),
        buffer(tiles, 8), buffer(tiles, 8), buffer(chunks, tiles, 64),
        buffer(2, chunks, tiles, 8 * CHUNK), buffer(tiles, 64),
        buffer(4, chunks, 2, lines // chunks), buffer(4, chunks, lines // chunks),
        dma((3, chunks, 4)), dma((3, chunks, 4)), dma((4,)), dma((4,)), dma((SUBSTEPS, 2)), dma((SUBSTEPS, 2)),
        dma, dma, dma((chunks,)), dma((chunks,)),
        dma((chunks, 4)), dma((chunks, 4)), dma((chunks, 4)), dma((chunks,)),
    ]
    result, integral = pl.pallas_call(
        functools.partial(kernel, nsuper, rows, tiles),
        out_shape=(jax.ShapeDtypeStruct((8, lines, LANES), f32), jax.ShapeDtypeStruct((lines, LANES), f32)),
        in_specs=[hbm] * 5,
        out_specs=(hbm, hbm),
        scratch_shapes=scratch,
        compiler_params=pltpu.CompilerParams(
            collective_id=0, has_side_effects=True, vmem_limit_bytes=60 * 2**20),
        name="transport_remap",
    )(in_lines(tracers), in_lines(courant_x), in_lines(courant_y), in_lines(thickness), level_weights)
    out, geo = pl.pallas_call(
        functools.partial(finish, rows, tiles),
        out_shape=(jax.ShapeDtypeStruct((8, lines, LANES), f32), jax.ShapeDtypeStruct((lines, LANES), f32)),
        in_specs=[hbm] * 3,
        out_specs=(hbm, hbm),
        scratch_shapes=[buffer(8, lines), buffer(lines), pltpu.VMEM((rows, nlon), f32), dma((2, 8)), dma((3,))],
        compiler_params=pltpu.CompilerParams(vmem_limit_bytes=60 * 2**20),
        name="finish",
    )(result, integral, surface_geo)
    return from_lines(out, levels, rows), from_lines(geo, levels, rows)


def solution(mesh):
    in_specs = (
        P(None, "lev", "lat", None),
        P("lev", "lat", None),
        P("lev", "lat", None),
        P("lev", "lat", None),
        P(),
        P("lat", None),
    )
    out_specs = (P(None, "lev", "lat", None), P("lev", "lat", None))
    run = functools.partial(body, mesh.shape["lat"] // 2)
    return jax.shard_map(run, mesh=mesh, in_specs=in_specs, out_specs=out_specs, check_vma=False)
```

time: 81.9 us -> 56.2 us (0.69)
  Pallas kernels: 74.9 us -> 55.4 us
  local copies, waits for them, and re-layouts: 6.14 us -> 0 us
    pallas_call x1 -> x2, Pallas kernels: 74.9 us -> 55.4 us  [the longest x1 53.1 us: body(): pl.pallas_call(functools.partial(kernel, nsuper, rows, tiles), out_shape=...]
    unnamed x8 -> x0, local copies, waits for them, and re-layouts: 4.07 us -> none
    pallas_call x2 -> x0, local copies, waits for them, and re-layouts: 2.07 us -> none  [body(): pl.pallas_call(functools.partial(kernel, nsuper, rows, nlon), out_shape=(...]
where the time goes in v1:
time: 56.2 us; the launch traced here: 56.1 us
  Pallas kernels  55.4 us (99%)
  between operations  0.64 us (1%)
    pallas_call x1, Pallas kernels, body(): pl.pallas_call(functools.partial(kernel, nsuper, rows, tiles), out_shape=...  53.1 us
    pallas_call x1, Pallas kernels, body(): pl.pallas_call(functools.partial(finish, rows, tiles), out_shape=(jax.Sha...  2.38 us

profile of v1, /device:TPU:111, one launch (start us, length us, event | category | flops | bytes accessed | tf_op | source)
XLA Modules:
  0.0 56.1 jit_solution(5913225673098863599)
XLA Ops:
  0.6 53.1 %transport_remap.1 = (f32[8,216,128]{2,1,0:T(8,128)}, f32[216,128]{1,0:T(8,128)}) custom-call(f32[8,216,128]{2,1,0:T(8,128)} %bitcast.30, f32[216,128]{1,0:T(8,128)} %bitcast.31, f32[216,128]{1,0:T(8,128)} %bitcast.32, f32[216,128]{1,0:T(8,128)} %bitcast.33, f32[8]{0:T(128)} %wts_hbm.1), custom_call_target="tpu_custom_call" | custom-call | tf_op jit(solution)/shard_map/transport_remap/pallas_call | solution.py:560
  53.7 2.4 %finish.1 = (f32[8,216,128]{2,1,0:T(8,128)}, f32[216,128]{1,0:T(8,128)}) custom-call(f32[8,216,128]{2,1,0:T(8,128)} %get-tuple-element.6.result, f32[216,128]{1,0:T(8,128)} %get-tuple-element.7.integral, f32[12,1152]{1,0:T(8,128)} %surface.1), custom_call_target="tpu_custom_call" | custom-call | tf_op jit(solution)/shard_map/finish/pallas_call | solution.py:570

commit v2 on v1

--- a/solution.py
+++ b/solution.py
@@ -14,6 +14,7 @@
 LANES = 128
 TOP_PRESSURE = 1.0
 GAS_FACTOR = 0.3
+SHIFTS = (-3, -2, 2, 3)
 
 
 def face_weights(courant):
@@ -40,7 +41,7 @@
 
 
 def kernel(nsuper, rows, tiles, tr, cx, cy, th, wts_hbm, out, geor, wts, lsem,
-           recvf, recvx, recvy, thr, field, zon, cxt, cyt, wz, wy, cyrow, cytop, tht, col, tmp, outp, geop,
+           recvf, recvx, recvy, thr, field, zon, cxt, cyt, wz, wy, cyrow, cytop, tht, col, tmp, outp, geop, turns,
            s1, r1, sth, rth, sh, rh, sc, rc, sx, rx, so, ro, sg, rg):
     lat, lev = lax.axis_index("lat"), lax.axis_index("lev")
     sb, l = lat // 2, lat % 2
@@ -77,6 +78,12 @@
         for t in range(SUBSTEPS):
             zon[t, :, 8 * (HALO + both):, :] = jnp.zeros((tiles, 8 * HALO, LANES), jnp.float32)
         cytop[...] = jnp.zeros((tiles, 8, LANES), jnp.float32)
+
+    source = lax.broadcasted_iota(jnp.int32, (2 * LANES, LANES), 0) % LANES
+    target = lax.broadcasted_iota(jnp.int32, (2 * LANES, LANES), 1)
+    for n, steps in enumerate(SHIFTS):
+        turns[:, n * LANES:(n + 1) * LANES] = jnp.where(
+            source == (target + (steps + LANES)) % LANES, 1.0, 0.0).astype(jnp.bfloat16)
 
     others = 7 + has_low.astype(jnp.int32) + has_up.astype(jnp.int32)
     pl.semaphore_wait(barrier, others)
@@ -146,8 +153,10 @@
     keep = jnp.where(has_low, 1.0, 0.0)
 
     def shifted(values, steps):
-        count = len(values)
-        turned = [pltpu.roll(v, (-steps) % LANES, 1) for v in values]
+        return merged([pltpu.roll(v, (-steps) % LANES, 1) for v in values], steps)
+
+    def merged(turned, steps):
+        count = len(turned)
         if steps < 0:
             return [jnp.where(col_id < -steps, turned[m - 1], turned[m]) for m in range(count)]
         return [jnp.where(col_id >= LANES - steps, turned[(m + 1) % count], turned[m]) for m in range(count)]
@@ -203,25 +212,30 @@
     def low_row():
         return copy_to(cyrow, cytop, sc, rc, (lat - 2, lev))
 
-    def zonal(t, starts, n, step):
-        def do(i, _):
-            for first in starts:
-                for d in range(step):
-                    row = first + i * step + d
-                    at8 = at_row(row)
-                    f = [field[t, m, at8, :] for m in range(tiles)]
-                    total = [wz[3, m, at8, :] * f[m] for m in range(tiles)]
-                    for k in (0, 1, 2, 4, 5, 6):
-                        moved = shifted(f, k - 3)
-                        total = [total[m] + wz[k, m, at8, :] * moved[m] for m in range(tiles)]
-                    to8 = at_row(row + HALO)
-                    for m in range(tiles):
-                        zon[t, m, to8, :] = total[m]
-            return 0
-        if n == step:
-            do(0, 0)
-        else:
-            lax.fori_loop(0, n // step, do, 0)
+    def zonal(t, rows_here):
+        f = [[field[t, m, at_row(row), :] for m in range(tiles)] for row in rows_here]
+        flat = jnp.concatenate([v for one in f for v in one], axis=0)
+        head = flat.astype(jnp.bfloat16)
+        rest = (flat - head.astype(jnp.float32)).astype(jnp.bfloat16)
+        parts = jnp.concatenate([head, rest], axis=1)
+        turned = {}
+        for n in range(0, len(SHIFTS), 2):
+            moved = jnp.dot(parts, turns[:, n * LANES:(n + 2) * LANES], preferred_element_type=jnp.float32)
+            turned[SHIFTS[n]], turned[SHIFTS[n + 1]] = moved[:, :LANES], moved[:, LANES:]
+        for n, row in enumerate(rows_here):
+            at8 = at_row(row)
+            total = [wz[3, m, at8, :] * f[n][m] for m in range(tiles)]
+            for k in (0, 1, 2, 4, 5, 6):
+                steps = k - 3
+                if steps in turned:
+                    first = 8 * tiles * n
+                    moved = merged([turned[steps][first + 8 * m:first + 8 * m + 8] for m in range(tiles)], steps)
+                else:
+                    moved = shifted(f[n], steps)
+                total = [total[m] + wz[k, m, at8, :] * moved[m] for m in range(tiles)]
+            to8 = at_row(row + HALO)
+            for m in range(tiles):
+                zon[t, m, to8, :] = total[m]
 
     def meridional(t, starts, n):
         def do(i, _):
@@ -250,7 +264,7 @@
                         sums = sums[1:] + [window[4] + window[5]]
                         values = values[1:] + [face(3)]
             return 0
-        lax.fori_loop(0, tiles, do, 0)
+        lax.fori_loop(0, tiles, do, 0, unroll=True)
 
     edge = 8 * HALO
     top = 8 * both
@@ -265,7 +279,7 @@
                        sh.at[t, 1], rh.at[t, 1], (lat + 2, lev))
 
     def send_halo(t):
-        zonal(t, ends, HALO, HALO)
+        zonal(t, [first + d for first in ends for d in range(HALO)])
 
         @pl.when(has_low)
         def _():
@@ -404,7 +418,7 @@
 
     take_fields(0)
     send_halo(0)
-    zonal(0, [HALO, both - HALO - 1], 1, 1)
+    zonal(0, [HALO, both - HALO - 1])
     take_courant(0)
 
     @pl.when(has_low)
@@ -412,7 +426,7 @@
         low_row().start()
 
     take_fields(1)
-    zonal(0, both_places(1), CHUNK, CHUNK)
+    zonal(0, [first + d for first in both_places(1) for d in range(CHUNK)])
     take_courant(1)
 
     @pl.when(has_up)
@@ -423,20 +437,21 @@
     wait_halo(0)
     meridional(0, [0, both - 5], 5)
     send_halo(1)
-    zonal(1, [HALO, both - 5], 2, 2)
+    zonal(1, [3, 4, both - 5, both - 4])
 
     take_fields(2)
-    zonal(0, both_places(2), CHUNK, CHUNK)
+    zonal(0, list(range(8, 16)))
     take_courant(2)
     meridional(0, [5], both - 10)
-    zonal(1, [5, 12], 7, 1)
+    zonal(1, list(range(5, 19)))
     wait_halo(1)
     meridional(1, ends, HALO)
     send_halo(2)
     meridional(1, [HALO], both - 2 * HALO)
-    zonal(2, [HALO], both - 2 * HALO, 6)
+    zonal(2, list(range(3, 13)))
+    zonal(2, list(range(13, 21)))
     meridional(2, [5], both - 10)
-    zonal(3, [5, 12], 7, 1)
+    zonal(3, list(range(5, 19)))
     meridional(3, [8], 8)
     send_swap(2)
 
@@ -446,7 +461,7 @@
     take_thickness()
     send_results(2)
     meridional(2, [HALO, both - 5], 2)
-    zonal(3, [HALO, both - 5], 2, 2)
+    zonal(3, [3, 4, both - 5, both - 4])
     meridional(3, [HALO, both - 8], 5)
     send_swap(1)
     send_results(1)
@@ -553,6 +568,7 @@
         buffer(tiles, 8), buffer(tiles, 8), buffer(chunks, tiles, 64),
         buffer(2, chunks, tiles, 8 * CHUNK), buffer(tiles, 64),
         buffer(4, chunks, 2, lines // chunks), buffer(4, chunks, lines // chunks),
+        pltpu.VMEM((2 * LANES, len(SHIFTS) * LANES), jnp.bfloat16),
         dma((3, chunks, 4)), dma((3, chunks, 4)), dma((4,)), dma((4,)), dma((SUBSTEPS, 2)), dma((SUBSTEPS, 2)),
         dma, dma, dma((chunks,)), dma((chunks,)),
         dma((chunks, 4)), dma((chunks, 4)), dma((chunks, 4)), dma((chunks,)),

time: 56.2 us -> 54.8 us (0.975)
  Pallas kernels: 55.4 us -> 53.6 us
    pallas_call x1, Pallas kernels: 53.1 us -> 51.3 us  [body(): pl.pallas_call(functools.partial(kernel, nsuper, rows, tiles), out_shape=...]
where the time goes in v2:
time: 54.8 us; the launch traced here: 54.3 us
  Pallas kernels  53.6 us (98%)
  between operations  0.64 us (1%)
    pallas_call x1, Pallas kernels, body(): pl.pallas_call(functools.partial(kernel, nsuper, rows, tiles), out_shape=...  51.3 us
    pallas_call x1, Pallas kernels, body(): pl.pallas_call(functools.partial(finish, rows, tiles), out_shape=(jax.Sha...  2.38 us

profile of v2, /device:TPU:111, one launch (start us, length us, event | category | flops | bytes accessed | tf_op | source)
XLA Modules:
  0.0 54.3 jit_solution(17801812884564152958)
XLA Ops:
  0.6 51.3 %transport_remap.1 = (f32[8,216,128]{2,1,0:T(8,128)}, f32[216,128]{1,0:T(8,128)}) custom-call(f32[8,216,128]{2,1,0:T(8,128)} %bitcast.30, f32[216,128]{1,0:T(8,128)} %bitcast.31, f32[216,128]{1,0:T(8,128)} %bitcast.32, f32[216,128]{1,0:T(8,128)} %bitcast.33, f32[8]{0:T(128)} %wts_hbm.1), custom_call_target="tpu_custom_call" | custom-call | tf_op jit(solution)/shard_map/transport_remap/pallas_call | solution.py:576
  51.9 2.4 %finish.1 = (f32[8,216,128]{2,1,0:T(8,128)}, f32[216,128]{1,0:T(8,128)}) custom-call(f32[8,216,128]{2,1,0:T(8,128)} %get-tuple-element.6.result, f32[216,128]{1,0:T(8,128)} %get-tuple-element.7.integral, f32[12,1152]{1,0:T(8,128)} %surface.1), custom_call_target="tpu_custom_call" | custom-call | tf_op jit(solution)/shard_map/finish/pallas_call | solution.py:586

commit v3 on v2

--- a/solution.py
+++ b/solution.py
@@ -40,9 +40,9 @@
     ]
 
 
-def kernel(nsuper, rows, tiles, tr, cx, cy, th, wts_hbm, out, geor, wts, lsem,
+def kernel(nsuper, rows, tiles, tr, cx, cy, th, wts_hbm, out, above, span_out, wts, lsem, spans,
            recvf, recvx, recvy, thr, field, zon, cxt, cyt, wz, wy, cyrow, cytop, tht, col, tmp, outp, geop, turns,
-           s1, r1, sth, rth, sh, rh, sc, rc, sx, rx, so, ro, sg, rg):
+           s1, r1, sth, rth, sh, rh, sc, rc, sx, rx, so, ro, sg, rg, sp):
     lat, lev = lax.axis_index("lat"), lax.axis_index("lev")
     sb, l = lat // 2, lat % 2
     h, c = lev // 2, lev % 2
@@ -339,8 +339,22 @@
                     piece = thr[k // 2, pl.ds(first + k % 2, CHUNK, stride=pitch), :]
                     for f in range(2):
                         tht[j, i, pl.ds(8 * k + f, CHUNK, stride=2), :] = piece
+            for r0, n in ((0, 8), (8, rows - 8)):
+                total = None
+                for k in range(8):
+                    piece = thr[k // 2, pl.ds(r0 * pitch + 2 * i + k % 2, n, stride=pitch), :]
+                    total = piece if total is None else total + piece
+                spans[pl.ds(r0 * tiles + i, n, stride=tiles), :] = total
             return 0
         lax.fori_loop(0, tiles, do, 0)
+
+        @pl.when(c == l)
+        def _():
+            keep_spans.start()
+            give_spans.start()
+
+    keep_spans = pltpu.make_async_copy(spans, span_out, sp.at[0])
+    give_spans = copy_to(spans, span_out, sp.at[1], sp.at[2], (lat, lev ^ 1))
 
     def columns(j, i):
         weights = [jnp.full(full, wts[k], jnp.float32) for k in range(8)]
@@ -369,11 +383,11 @@
                 for n in range(8):
                     cut = jnp.maximum(0.0, jnp.minimum(bounds[n + 1], low[k]) - jnp.maximum(bounds[n], up[k]))
                     total = density[n] * cut if total is None else total + density[n] * cut
-                tmp[i, 8 * k:8 * k + 8, :] = total
+                tmp[j, i, 8 * k:8 * k + 8, :] = total
             for k in range(8):
                 for f in range(2):
                     outp[k // 2, j, f, pl.ds(2 * i + k % 2, CHUNK, stride=pitch), :] = (
-                        tmp[i, pl.ds(8 * k + f, CHUNK, stride=2), :])
+                        tmp[j, i, pl.ds(8 * k + f, CHUNK, stride=2), :])
             return 0
         lax.fori_loop(0, tiles, do, 0)
 
@@ -382,12 +396,11 @@
             _, _, low, up = columns(j, i)
             total = None
             for k in range(7, -1, -1):
-                layer = GAS_FACTOR * tmp[i, 8 * k:8 * k + 8, :] / (low[k] - up[k]) * jnp.log(low[k] / up[k])
+                layer = GAS_FACTOR * tmp[j, i, 8 * k:8 * k + 8, :] / (low[k] - up[k]) * jnp.log(low[k] / up[k])
                 total = layer if total is None else total + layer
-                tmp[i, 8 * k:8 * k + 8, :] = total
-            for k in range(8):
-                geop[k // 2, j, pl.ds(2 * i + k % 2, CHUNK, stride=pitch), :] = (
-                    tmp[i, pl.ds(8 * k, CHUNK, stride=2), :])
+                tmp[j, i, 8 * k:8 * k + 8, :] = total
+            for n in range(3):
+                geop[n, j, pl.ds(i, CHUNK, stride=tiles), :] = tmp[j, i, pl.ds(8 * (2 * n + 2), CHUNK, stride=2), :]
             return 0
         lax.fori_loop(0, tiles, do, 0)
 
@@ -399,10 +412,8 @@
                    so.at[j, k], ro.at[j, y], (2 * sb + c, gd))
 
     def integral_moves(j):
-        here = span_of(c, j)
-        for k in (3, 2, 1, 0):
-            gd = lev ^ k
-            yield (None if k else (c == l), geop.at[gd, j], geor.at[here], sg.at[j, k], rg.at[j], (2 * sb + c, gd))
+        for n in range(3):
+            yield (None if n else (c == 0), geop.at[n, j], above.at[j], sg.at[j, n], rg.at[j], (2 * sb + c, n))
 
     def send_results(j):
         swap(j).wait_recv()
@@ -410,11 +421,13 @@
         for move in result_moves(j):
             start(*move)
 
+    def send_integrals(*which):
         @pl.when(y == 0)
         def _():
-            integrate(j)
-            for move in integral_moves(j):
-                start(*move)
+            for j in which:
+                integrate(j)
+                for move in integral_moves(j):
+                    start(*move)
 
     take_fields(0)
     send_halo(0)
@@ -455,24 +468,39 @@
     meridional(3, [8], 8)
     send_swap(2)
 
+    take_thickness()
+
     wait_halo(2)
     meridional(2, ends, HALO)
     send_halo(3)
-    take_thickness()
     send_results(2)
     meridional(2, [HALO, both - 5], 2)
     zonal(3, [3, 4, both - 5, both - 4])
     meridional(3, [HALO, both - 8], 5)
     send_swap(1)
+    send_integrals(2)
     send_results(1)
 
     wait_halo(3)
     meridional(3, ends, HALO)
     send_swap(0)
+    send_integrals(1)
     send_results(0)
-
-    for j in range(chunks):
-        arrived(geor.at[span_of(l, j)], rg.at[j])
+    send_integrals(0)
+
+    @pl.when(lev < 3)
+    def _():
+        for j in range(chunks):
+            arrived(above.at[j], rg.at[j])
+
+    @pl.when(c == l)
+    def _():
+        keep_spans.wait()
+        give_spans.wait_send()
+
+    @pl.when(c != l)
+    def _():
+        give_spans.wait_recv()
     for j in range(chunks):
         for s in range(4):
             arrived(out.at[pl.ds(2 * s, 2), span_of(l, j)], ro.at[j, s])
@@ -502,24 +530,48 @@
             to_up(t).wait_send()
 
 
-def finish(rows, tiles, result, integral, surface, out, geo, held, total, sgeo, sems, gsems):
-    loads = [pltpu.make_async_copy(integral, total, gsems.at[0]), pltpu.make_async_copy(surface, sgeo, gsems.at[1])]
+def finish(rows, tiles, result, above, span_in, wts, surface, out, geo, held, over, spans, sgeo, sums, total, sems, gsems):
+    lat, lev = lax.axis_index("lat"), lax.axis_index("lev")
+    l = lat % 2
+    pitch = 2 * tiles
+    loads = [pltpu.make_async_copy(above, over, gsems.at[0]), pltpu.make_async_copy(span_in, spans, gsems.at[1]),
+             pltpu.make_async_copy(surface, sgeo, gsems.at[2])]
     takes = [pltpu.make_async_copy(result.at[f], held.at[f], sems.at[0, f]) for f in range(8)]
     gives = [pltpu.make_async_copy(held.at[f], out.at[f], sems.at[1, f]) for f in range(8)]
-    for copy in loads + takes:
+    for copy in takes[:1] + loads + takes[1:]:
         copy.start()
     for copy in loads:
         copy.wait()
-    pitch = 2 * tiles
-    for i in range(tiles):
-        for r0, n in ((0, 8), (8, rows - 8)):
-            piece = sgeo[r0:r0 + n, i * LANES:(i + 1) * LANES]
-            for a in range(2):
+    takes[0].wait()
+    gives[0].start()
+    for j in range(rows // CHUNK):
+        row = jnp.where(l == 0, j * CHUNK, rows - (j + 1) * CHUNK)
+        for i in range(tiles):
+            sums[pl.ds(row * tiles + i, CHUNK, stride=tiles), :] = over[j, pl.ds(i, CHUNK, stride=tiles), :]
+    for r0, n in ((0, 8), (8, rows - 8)):
+        shape = (n, LANES)
+        whole, below, mine = None, jnp.zeros(shape, jnp.float32), [None, None]
+        for k in range(8):
+            weight = jnp.full(shape, wts[k], jnp.float32)
+            whole = weight if whole is None else whole + weight
+            below = below + jnp.where(k < 2 * lev, weight, 0.0)
+            mine[k % 2] = weight if k < 2 else jnp.where(k // 2 == lev, weight, mine[k % 2])
+        inverse = 1.0 / whole
+        shares = [mine[0] * inverse, mine[1] * inverse]
+        fractions = [(below + mine[0]) * inverse, (below + mine[0] + mine[1]) * inverse]
+        for i in range(tiles):
+            span = spans[pl.ds(r0 * tiles + i, n, stride=tiles), :]
+            value = jnp.where(lev < 3, sums[pl.ds(r0 * tiles + i, n, stride=tiles), :], 0.0)
+            value = value + sgeo[r0:r0 + n, i * LANES:(i + 1) * LANES]
+            for a in (1, 0):
                 here = pl.ds(r0 * pitch + 2 * i + a, n, stride=pitch)
-                total[here, :] = total[here, :] + piece
-    store = pltpu.make_async_copy(total, geo, gsems.at[2])
+                low = TOP_PRESSURE + span * fractions[a]
+                up = low - span * shares[a]
+                value = value + GAS_FACTOR * held[0, here, :] / (low - up) * jnp.log(low / up)
+                total[here, :] = value
+    store = pltpu.make_async_copy(total, geo, gsems.at[3])
     store.start()
-    for take, give in zip(takes, gives):
+    for take, give in zip(takes[1:], gives[1:]):
         take.wait()
         give.start()
     for copy in gives + [store]:
@@ -554,30 +606,34 @@
     both = 2 * rows
     lines = rows * tiles * levels
     chunks = rows // CHUNK
+    sum_lines = -(-CHUNK * tiles // 8) * 8
+    span_lines = -(-rows * tiles // 8) * 8
 
     def buffer(*shape):
         return pltpu.VMEM(shape + (LANES,), f32)
 
     dma = pltpu.SemaphoreType.DMA
     scratch = [
-        pltpu.SMEM((8,), f32), dma,
+        pltpu.SMEM((8,), f32), dma, buffer(span_lines),
         buffer(4, 2, lines), buffer(4, lines), buffer(4, lines), buffer(4, lines),
         buffer(SUBSTEPS + 1, tiles, 8 * both), buffer(SUBSTEPS, tiles, 8 * (both + 2 * HALO)),
         buffer(tiles, 8 * both), buffer(tiles, 8 * both),
         buffer(7, tiles, 8 * both), buffer(3, tiles, 8 * (both + 1)),
         buffer(tiles, 8), buffer(tiles, 8), buffer(chunks, tiles, 64),
-        buffer(2, chunks, tiles, 8 * CHUNK), buffer(tiles, 64),
-        buffer(4, chunks, 2, lines // chunks), buffer(4, chunks, lines // chunks),
+        buffer(2, chunks, tiles, 8 * CHUNK), buffer(chunks, tiles, 64),
+        buffer(4, chunks, 2, lines // chunks), buffer(3, chunks, sum_lines),
         pltpu.VMEM((2 * LANES, len(SHIFTS) * LANES), jnp.bfloat16),
         dma((3, chunks, 4)), dma((3, chunks, 4)), dma((4,)), dma((4,)), dma((SUBSTEPS, 2)), dma((SUBSTEPS, 2)),
         dma, dma, dma((chunks,)), dma((chunks,)),
-        dma((chunks, 4)), dma((chunks, 4)), dma((chunks, 4)), dma((chunks,)),
+        dma((chunks, 4)), dma((chunks, 4)), dma((chunks, 3)), dma((chunks,)), dma((3,)),
     ]
-    result, integral = pl.pallas_call(
+    results = jax.ShapeDtypeStruct((8, lines, LANES), f32)
+    result, above, spans = pl.pallas_call(
         functools.partial(kernel, nsuper, rows, tiles),
-        out_shape=(jax.ShapeDtypeStruct((8, lines, LANES), f32), jax.ShapeDtypeStruct((lines, LANES), f32)),
+        out_shape=(results, jax.ShapeDtypeStruct((chunks, sum_lines, LANES), f32),
+                   jax.ShapeDtypeStruct((span_lines, LANES), f32)),
         in_specs=[hbm] * 5,
-        out_specs=(hbm, hbm),
+        out_specs=(hbm, hbm, hbm),
         scratch_shapes=scratch,
         compiler_params=pltpu.CompilerParams(
             collective_id=0, has_side_effects=True, vmem_limit_bytes=60 * 2**20),
@@ -585,13 +641,14 @@
     )(in_lines(tracers), in_lines(courant_x), in_lines(courant_y), in_lines(thickness), level_weights)
     out, geo = pl.pallas_call(
         functools.partial(finish, rows, tiles),
-        out_shape=(jax.ShapeDtypeStruct((8, lines, LANES), f32), jax.ShapeDtypeStruct((lines, LANES), f32)),
-        in_specs=[hbm] * 3,
+        out_shape=(results, jax.ShapeDtypeStruct((lines, LANES), f32)),
+        in_specs=[hbm] * 3 + [pl.BlockSpec(memory_space=pltpu.SMEM), hbm],
         out_specs=(hbm, hbm),
-        scratch_shapes=[buffer(8, lines), buffer(lines), pltpu.VMEM((rows, nlon), f32), dma((2, 8)), dma((3,))],
+        scratch_shapes=[buffer(8, lines), buffer(chunks, sum_lines), buffer(span_lines), pltpu.VMEM((rows, nlon), f32),
+                        buffer(span_lines), buffer(lines), dma((2, 8)), dma((4,))],
         compiler_params=pltpu.CompilerParams(vmem_limit_bytes=60 * 2**20),
         name="finish",
-    )(result, integral, surface_geo)
+    )(result, above, spans, level_weights, surface_geo)
     return from_lines(out, levels, rows), from_lines(geo, levels, rows)
 
 

time: 54.8 us -> 52.9 us (0.965)
  Pallas kernels: 53.6 us -> 51.4 us
    pallas_call x1, Pallas kernels: 51.3 us -> 48.2 us  [body(): pl.pallas_call(functools.partial(kernel, nsuper, rows, tiles), out_shape=...]
    pallas_call x1, Pallas kernels: 2.38 us -> 3.12 us  [body(): pl.pallas_call(functools.partial(finish, rows, tiles), out_shape=(results...]
where the time goes in v3:
time: 52.9 us; the launch traced here: 52 us
  Pallas kernels  51.4 us (97%)
  between operations  0.64 us (1%)
    pallas_call x1, Pallas kernels, body(): pl.pallas_call(functools.partial(kernel, nsuper, rows, tiles), out_shape=...  48.2 us
    pallas_call x1, Pallas kernels, body(): pl.pallas_call(functools.partial(finish, rows, tiles), out_shape=(results...  3.12 us

profile of v3, /device:TPU:111, one launch (start us, length us, event | category | flops | bytes accessed | tf_op | source)
XLA Modules:
  0.0 52.0 jit_solution(7582650883017426554)
XLA Ops:
  0.6 48.2 %transport_remap.1 = (f32[8,216,128]{2,1,0:T(8,128)}, f32[3,40,128]{2,1,0:T(8,128)}, f32[112,128]{1,0:T(8,128)}) custom-call(f32[8,216,128]{2,1,0:T(8,128)} %bitcast.30, f32[216,128]{1,0:T(8,128)} %bitcast.31, f32[216,128]{1,0:T(8,128)} %bitcast.32, f32[216,128]{1,0:T(8,128)} %bitcast.33, f32[8]{0:T(128)} %wts.1), custom_call_target="tpu_custom_call" | custom-call | tf_op jit(solution)/shard_map/transport_remap/pallas_call | solution.py:631
  48.9 3.1 %finish.1 = (f32[8,216,128]{2,1,0:T(8,128)}, f32[216,128]{1,0:T(8,128)}) custom-call(f32[8,216,128]{2,1,0:T(8,128)} %get-tuple-element.7.result, f32[3,40,128]{2,1,0:T(8,128)} %get-tuple-element.8.above, f32[112,128]{1,0:T(8,128)} %get-tuple-element.9.span_in, f32[8]{0:T(128)} %wts.1, f32[12,1152]{1,0:T(8,128)} %surface.1), custom_call_target="tpu_custom_call" | custom-call | tf_op jit(solution)/shard_map/finish/pallas_call | solution.py:642

commit v4 on v3

--- a/solution.py
+++ b/solution.py
@@ -42,7 +42,7 @@
 
 def kernel(nsuper, rows, tiles, tr, cx, cy, th, wts_hbm, out, above, span_out, wts, lsem, spans,
            recvf, recvx, recvy, thr, field, zon, cxt, cyt, wz, wy, cyrow, cytop, tht, col, tmp, outp, geop, turns,
-           s1, r1, sth, rth, sh, rh, sc, rc, sx, rx, so, ro, sg, rg, sp):
+           s1, r1, sth, rth, sh, rh, sc, rc, sx, rx, so, ro, sg, rg, sp, fw):
     lat, lev = lax.axis_index("lat"), lax.axis_index("lev")
     sb, l = lat // 2, lat % 2
     h, c = lev // 2, lev % 2
@@ -125,28 +125,46 @@
         first = place(band, j) * pitch
         return pl.ds(first if isinstance(first, int) else pl.multiple_of(first, 8), lines)
 
-    moves = []
+    courant_moves, field_moves = [], []
     slot = 2 * l + c
     for j in range(chunks):
         here = span_of(l, j)
-        groups = [[], [], []]
+        courant_moves.append([])
+        field_moves.append([])
         for k in (3, 2, 1, 0):
             hd, ld = h ^ (k // 2), l ^ (k % 2)
             own = None if k else (c == h)
             device = (2 * sb + ld, 2 * hd + h)
-            groups[0].append((own, tr.at[pl.ds(2 * (2 * hd + ld), 2), here], recvf.at[slot, :, here],
-                              s1.at[0, j, k], r1.at[0, j, slot], device))
-            groups[1].append((own, cx.at[here], recvx.at[slot, here], s1.at[1, j, k], r1.at[1, j, slot], device))
-            groups[2].append((own, cy.at[here], recvy.at[slot, here], s1.at[2, j, k], r1.at[2, j, slot], device))
-        for group in groups:
-            moves += group
+            field_moves[j].append((own, tr.at[pl.ds(2 * (2 * hd + ld), 2), here], recvf.at[slot, :, here],
+                                   s1.at[0, j, k], r1.at[0, j, slot], device))
+            if k != 2:
+                for kind, ref, target in ((1, cx, recvx), (2, cy, recvy)):
+                    courant_moves[j].append((own, ref.at[here], target.at[slot, here],
+                                             s1.at[kind, j, k], r1.at[kind, j, slot], device))
+    thick_moves = []
     for k in (3, 2, 1, 0):
         hd, ld = h ^ (k // 2), l ^ (k % 2)
         own = None if k else (c == l)
-        moves.append((own, th, thr.at[lev], sth.at[k], rth.at[lev], (2 * sb + ld, 2 * hd + l)))
-    for move in moves:
-        start(*move)
-
+        thick_moves.append((own, th, thr.at[lev], sth.at[k], rth.at[lev], (2 * sb + ld, 2 * hd + l)))
+
+    passed = 2 * (1 - l) + (h ^ c)
+
+    def forward(kind, j):
+        ref = (recvx if kind == 1 else recvy).at[passed, span_of(1 - l, j)]
+        return copy_to(ref, ref, fw.at[kind - 1, j], r1.at[kind, j, passed], (2 * sb + 1 - l, 2 * (1 - c) + c))
+
+    def pass_on(j):
+        for kind in (1, 2):
+            ref = (recvx if kind == 1 else recvy).at[passed, span_of(1 - l, j)]
+            arrived(ref, r1.at[kind, j, passed])
+            forward(kind, j).start()
+
+    def start_all(*groups):
+        for group in groups:
+            for move in group:
+                start(*move)
+
+    start_all(courant_moves[0], field_moves[0], courant_moves[1])
     weights_copy.wait()
 
     col_id = lax.broadcasted_iota(jnp.int32, (8, LANES), 1)
@@ -299,20 +317,18 @@
             to_low(t).wait_recv()
 
     def take_fields(j):
-        for kind, ref in ((0, recvf), (1, recvx)):
+        for s in range(4):
+            arrived(recvf.at[s, :, span_of(s // 2, j)], r1.at[0, j, s])
+        unpack(j, recvf, field.at[0], False)
+
+    def take_courant(j):
+        for kind, ref, target in ((1, recvx, cxt), (2, recvy, cyt)):
             for s in range(4):
-                for band in range(2):
-                    if s // 2 == band:
-                        here = span_of(band, j)
-                        arrived(ref.at[s, :, here] if kind == 0 else ref.at[s, here], r1.at[kind, j, s])
-        unpack(j, recvx, cxt, True)
-        unpack(j, recvf, field.at[0], False)
+                @pl.when(s != passed)
+                def _():
+                    arrived(ref.at[s, span_of(s // 2, j)], r1.at[kind, j, s])
+            unpack(j, ref, target, True)
         zonal_weights(j)
-
-    def take_courant(j):
-        for s in range(4):
-            arrived(recvy.at[s, span_of(s // 2, j)], r1.at[2, j, s])
-        unpack(j, recvy, cyt, True)
         meridional_weights(j)
 
     part = 8 * CHUNK
@@ -429,18 +445,23 @@
                 for move in integral_moves(j):
                     start(*move)
 
+    pass_on(0)
+    start_all(courant_moves[2], field_moves[1])
+    take_courant(0)
+
+    @pl.when(has_low)
+    def _():
+        low_row().start()
     take_fields(0)
     send_halo(0)
+    pass_on(1)
     zonal(0, [HALO, both - HALO - 1])
-    take_courant(0)
-
-    @pl.when(has_low)
-    def _():
-        low_row().start()
-
+    pass_on(2)
+    start_all(field_moves[2], thick_moves)
+
+    take_courant(1)
     take_fields(1)
     zonal(0, [first + d for first in both_places(1) for d in range(CHUNK)])
-    take_courant(1)
 
     @pl.when(has_up)
     def _():
@@ -452,9 +473,9 @@
     send_halo(1)
     zonal(1, [3, 4, both - 5, both - 4])
 
+    take_courant(2)
     take_fields(2)
     zonal(0, list(range(8, 16)))
-    take_courant(2)
     meridional(0, [5], both - 10)
     zonal(1, list(range(5, 19)))
     wait_halo(1)
@@ -469,11 +490,11 @@
     send_swap(2)
 
     take_thickness()
+    send_results(2)
 
     wait_halo(2)
     meridional(2, ends, HALO)
     send_halo(3)
-    send_results(2)
     meridional(2, [HALO, both - 5], 2)
     zonal(3, [3, 4, both - 5, both - 4])
     meridional(3, [HALO, both - 8], 5)
@@ -505,8 +526,12 @@
         for s in range(4):
             arrived(out.at[pl.ds(2 * s, 2), span_of(l, j)], ro.at[j, s])
 
-    for move in moves:
-        sent(*move)
+    for group in courant_moves + field_moves + [thick_moves]:
+        for move in group:
+            sent(*move)
+    for j in range(chunks):
+        for kind in (1, 2):
+            forward(kind, j).wait_send()
     for j in range(chunks):
         swap(j).wait_send()
         for move in result_moves(j):
@@ -625,7 +650,7 @@
         pltpu.VMEM((2 * LANES, len(SHIFTS) * LANES), jnp.bfloat16),
         dma((3, chunks, 4)), dma((3, chunks, 4)), dma((4,)), dma((4,)), dma((SUBSTEPS, 2)), dma((SUBSTEPS, 2)),
         dma, dma, dma((chunks,)), dma((chunks,)),
-        dma((chunks, 4)), dma((chunks, 4)), dma((chunks, 3)), dma((chunks,)), dma((3,)),
+        dma((chunks, 4)), dma((chunks, 4)), dma((chunks, 3)), dma((chunks,)), dma((3,)), dma((2, chunks)),
     ]
     results = jax.ShapeDtypeStruct((8, lines, LANES), f32)
     result, above, spans = pl.pallas_call(

time: 52.9 us -> 52.7 us (level)
  no operation moved by 1% of the time
where the time goes in v4:
time: 52.7 us; the launch traced here: 51.9 us
  Pallas kernels  51.2 us (97%)
  between operations  0.64 us (1%)
    pallas_call x1, Pallas kernels, body(): pl.pallas_call(functools.partial(kernel, nsuper, rows, tiles), out_shape=...  48.1 us
    pallas_call x1, Pallas kernels, body(): pl.pallas_call(functools.partial(finish, rows, tiles), out_shape=(results...  3.12 us

profile of v4, /device:TPU:111, one launch (start us, length us, event | category | flops | bytes accessed | tf_op | source)
XLA Modules:
  0.0 51.9 jit_solution(18022860120971779286)
XLA Ops:
  0.6 48.1 %transport_remap.1 = (f32[8,216,128]{2,1,0:T(8,128)}, f32[3,40,128]{2,1,0:T(8,128)}, f32[112,128]{1,0:T(8,128)}) custom-call(f32[8,216,128]{2,1,0:T(8,128)} %bitcast.30, f32[216,128]{1,0:T(8,128)} %bitcast.31, f32[216,128]{1,0:T(8,128)} %bitcast.32, f32[216,128]{1,0:T(8,128)} %bitcast.33, f32[8]{0:T(128)} %wts.1), custom_call_target="tpu_custom_call" | custom-call | tf_op jit(solution)/shard_map/transport_remap/pallas_call | solution.py:656
  48.7 3.1 %finish.1 = (f32[8,216,128]{2,1,0:T(8,128)}, f32[216,128]{1,0:T(8,128)}) custom-call(f32[8,216,128]{2,1,0:T(8,128)} %get-tuple-element.7.result, f32[3,40,128]{2,1,0:T(8,128)} %get-tuple-element.8.above, f32[112,128]{1,0:T(8,128)} %get-tuple-element.9.span_in, f32[8]{0:T(128)} %wts.1, f32[12,1152]{1,0:T(8,128)} %surface.1), custom_call_target="tpu_custom_call" | custom-call | tf_op jit(solution)/shard_map/finish/pallas_call | solution.py:667

commit v5 on v4

--- a/solution.py
+++ b/solution.py
@@ -565,10 +565,11 @@
     gives = [pltpu.make_async_copy(held.at[f], out.at[f], sems.at[1, f]) for f in range(8)]
     for copy in takes[:1] + loads + takes[1:]:
         copy.start()
+    for take, give in zip(takes, gives):
+        take.wait()
+        give.start()
     for copy in loads:
         copy.wait()
-    takes[0].wait()
-    gives[0].start()
     for j in range(rows // CHUNK):
         row = jnp.where(l == 0, j * CHUNK, rows - (j + 1) * CHUNK)
         for i in range(tiles):
@@ -596,9 +597,6 @@
                 total[here, :] = value
     store = pltpu.make_async_copy(total, geo, gsems.at[3])
     store.start()
-    for take, give in zip(takes[1:], gives[1:]):
-        take.wait()
-        give.start()
     for copy in gives + [store]:
         copy.wait()
 

time: 52.7 us -> 52.5 us (level)
  no operation moved by 1% of the time
where the time goes in v5:
time: 52.5 us; the launch traced here: 51.6 us
  Pallas kernels  51 us (97%)
  between operations  0.64 us (1%)
    pallas_call x1, Pallas kernels, body(): pl.pallas_call(functools.partial(kernel, nsuper, rows, tiles), out_shape=...  48.1 us
    pallas_call x1, Pallas kernels, body(): pl.pallas_call(functools.partial(finish, rows, tiles), out_shape=(results...  2.9 us

profile of v5, /device:TPU:111, one launch (start us, length us, event | category | flops | bytes accessed | tf_op | source)
XLA Modules:
  0.0 51.6 jit_solution(4461299689036775177)
XLA Ops:
  0.6 48.1 %transport_remap.1 = (f32[8,216,128]{2,1,0:T(8,128)}, f32[3,40,128]{2,1,0:T(8,128)}, f32[112,128]{1,0:T(8,128)}) custom-call(f32[8,216,128]{2,1,0:T(8,128)} %bitcast.30, f32[216,128]{1,0:T(8,128)} %bitcast.31, f32[216,128]{1,0:T(8,128)} %bitcast.32, f32[216,128]{1,0:T(8,128)} %bitcast.33, f32[8]{0:T(128)} %wts.1), custom_call_target="tpu_custom_call" | custom-call | tf_op jit(solution)/shard_map/transport_remap/pallas_call | solution.py:654
  48.7 2.9 %finish.1 = (f32[8,216,128]{2,1,0:T(8,128)}, f32[216,128]{1,0:T(8,128)}) custom-call(f32[8,216,128]{2,1,0:T(8,128)} %get-tuple-element.7.result, f32[3,40,128]{2,1,0:T(8,128)} %get-tuple-element.8.above, f32[112,128]{1,0:T(8,128)} %get-tuple-element.9.span_in, f32[8]{0:T(128)} %wts.1, f32[12,1152]{1,0:T(8,128)} %surface.1), custom_call_target="tpu_custom_call" | custom-call | tf_op jit(solution)/shard_map/finish/pallas_call | solution.py:665
